TPU v7x, 256 devices: a whole 4x4x8 slice. The times are simulated.
256 devices in a mesh: grp: 4 (over y), dev: 64 (over x, z, core).
Axes of the slice: x: 4, y: 4, z: 8, core: 2. Of those that a mesh axis runs over, the one named last changes fastest.
Arguments:
- enc_states: bfloat16 [128, 96, 2048], P('dev'), may hold values from -6 to 6
- norm_gain: float32 [2048], replicated, may hold values from 0.4 to 1.6
- final_gain: float32 [2048], replicated, may hold values from 0.4 to 1.6
- expert_ids: int32 [128, 96, 2], P('dev'), may hold values from 0 to 63, all different within a row; in each aligned block of 192 rows (0 to 191, 192 to 383, ..., all dimensions but the last counted through in order) at most 8 rows name the same one
- expert_gates: float32 [128, 96, 2], P('dev'), may hold values from 0.2 to 1
- source_lengths: int32 [128], P('dev'), may hold values from 12 to 96, as said below
- w_in: bfloat16 [64, 2048, 4096], P('dev', None, 'grp'), may hold values from -0.125 to 0.125
- w_out: bfloat16 [64, 4096, 2048], P('dev', 'grp'), may hold values from -0.09375 to 0.09375
- w_key: bfloat16 [2048, 2048], P('dev', 'grp'), may hold values from -0.125 to 0.125
- w_value: bfloat16 [2048, 2048], P('dev', 'grp'), may hold values from -0.125 to 0.125
- cross_query: bfloat16 [128, 2048], P('dev', 'grp'), may hold values from -6 to 6
Outputs:
- encoded: bfloat16 [128, 96, 2048], P('dev')
- context: bfloat16 [128, 2048], P('dev', 'grp')
Inputs may be any that keep to these rules, and one draw needn't show every extreme that they name: `expert_ids`: among the 384 choices of the positions of one index of dev (padded positions included), no expert is named more than 8 times, a bound that some block reaches. `source_lengths`: some sentence has exactly 96 tokens.
All inputs are finite; a program needn't handle non-finite values.
Results may differ from a plain program's by a relative error of at most 0.017.
Values may be sent and summed in bfloat16 or wider, within the bound.
A program may use at most 64 MiB of HBM per device.

v0:
```python
import math

import jax
import jax.numpy as jnp
from jax import lax
from jax.sharding import PartitionSpec as P

HEADS = 16


norm_epsilon = 1e-05


def layer_norm(values, gain_vector):
    average = jnp.mean(values, axis=-1, keepdims=True)
    centered = values - average
    variance = jnp.mean(centered * centered, axis=-1, keepdims=True)
    return centered * lax.rsqrt(variance + norm_epsilon) * gain_vector


def on_device(
    enc_states,
    norm_gain,
    final_gain,
    expert_ids,
    expert_gates,
    source_lengths,
    w_in,
    w_out,
    w_key,
    w_value,
    cross_query,
):
    sentences, length, model_width = enc_states.shape
    row_count = sentences * length
    experts = lax.axis_size("dev")
    capacity = (2 * row_count + experts - 1) // experts + 2
    states = enc_states.reshape(row_count, model_width).astype(jnp.float32)
    normed = layer_norm(states, norm_gain).astype(jnp.bfloat16)
    positions = lax.broadcasted_iota(jnp.int32, (sentences, length), 1)
    live_mask = positions < source_lengths[:, None]
    live_pairs = jnp.repeat(live_mask.reshape(row_count), 2)
    chosen = expert_ids.reshape(2 * row_count)
    onehot = (
        (chosen[:, None] == jnp.arange(experts, dtype=jnp.int32)[None, :]) & live_pairs[:, None]
    ).astype(jnp.int32)
    before = jnp.cumsum(onehot, axis=0) - onehot
    slot_index = jnp.sum(before * onehot, axis=1)
    target = jnp.where(live_pairs, chosen * capacity + slot_index, experts * capacity)
    token_rows = jnp.arange(2 * row_count, dtype=jnp.int32) // 2
    dispatch_buffer = (
        jnp.zeros((experts * capacity, model_width), jnp.bfloat16)
        .at[target]
        .set(normed[token_rows], mode="drop")
    )
    dispatch_buffer = dispatch_buffer.reshape(experts, capacity, model_width)
    gate_pairs = expert_gates.reshape(2 * row_count) * live_pairs.astype(jnp.float32)
    safe_target = jnp.minimum(target, experts * capacity - 1)
    arrived = lax.all_to_all(dispatch_buffer, "dev", split_axis=0, concat_axis=0, tiled=True)
    flattened = arrived.reshape(-1, model_width)
    hidden = jnp.maximum(
        jnp.dot(flattened, w_in[0], preferred_element_type=jnp.float32), 0.0
    ).astype(jnp.bfloat16)
    outputs = jnp.dot(hidden, w_out[0], preferred_element_type=jnp.float32)
    returned = lax.all_to_all(
        outputs.reshape(arrived.shape[0], arrived.shape[1], model_width),
        "dev",
        split_axis=0,
        concat_axis=0,
        tiled=True,
    )
    feature_count = returned.shape[2]
    flat_back = returned.reshape(experts * capacity, feature_count)
    picked = flat_back[safe_target] * gate_pairs[:, None]
    mixture = lax.psum(jnp.sum(picked.reshape(row_count, 2, feature_count), axis=1), "grp")
    encoded = layer_norm(states + mixture, final_gain).astype(jnp.bfloat16)
    column_count = w_key.shape[1]
    key_rows = lax.all_gather(w_key, "dev", axis=0, tiled=True)
    value_rows = lax.all_gather(w_value, "dev", axis=0, tiled=True)
    key_sum = jnp.dot(encoded, key_rows, preferred_element_type=jnp.float32)
    value_sum = jnp.dot(encoded, value_rows, preferred_element_type=jnp.float32)
    head_dim = model_width // HEADS
    local_heads = column_count // head_dim
    key_cache = key_sum.astype(jnp.bfloat16).reshape(sentences, length, local_heads, head_dim)
    value_cache = value_sum.astype(jnp.bfloat16).reshape(sentences, length, local_heads, head_dim)
    queries = cross_query.reshape(sentences, local_heads, head_dim)
    scores = jnp.einsum("shd,sthd->sht", queries, key_cache, preferred_element_type=jnp.float32) * (
        1.0 / math.sqrt(head_dim)
    )
    weights = jnp.exp(scores) * live_mask[:, None, :].astype(jnp.float32)
    probabilities = (weights / jnp.sum(weights, axis=-1, keepdims=True)).astype(jnp.bfloat16)
    context = jnp.einsum(
        "sht,sthd->shd", probabilities, value_cache, preferred_element_type=jnp.float32
    )
    return (
        encoded.reshape(sentences, length, model_width),
        context.astype(jnp.bfloat16).reshape(sentences, column_count),
    )


def solution(mesh):
    return jax.shard_map(
        on_device,
        mesh=mesh,
        in_specs=(
            P("dev", None, None),
            P(),
            P(),
            P("dev", None, None),
            P("dev", None, None),
            P("dev"),
            P("dev", None, "grp"),
            P("dev", "grp", None),
            P("dev", "grp"),
            P("dev", "grp"),
            P("dev", "grp"),
        ),
        out_specs=(P("dev", None, None), P("dev", "grp")),
        check_vma=False,
    )
```

profile of v0, /device:TPU:1, one launch (start us, length us, event | category | flops | bytes accessed | tf_op | source)
XLA Modules:
  0.0 385.8 jit_solution(11671468645735214732)
XLA Ops:
  8.0 0.8 fusion.44
  9.0 0.8 copy.23
  10.2 0.1 and.35
  10.3 0.2 reshape.255
  10.5 0.7 broadcast_multiply_fusion
  11.2 1.3 convert_reduce_fusion
  12.5 1.5 multiply_reduce_fusion.2
  14.2 0.1 broadcast_in_dim.15
  14.4 0.9 reduce-window.6
  15.3 0.2 slice_reduce_fusion
  16.1 0.4 multiply_convert_fusion.1
  16.5 8.5 %scatter_custom_fusion = bf16[512,2048]{1,0:T(8,128)(2,1)S(1)} fusion(s32[384]{0:T(512)S(1)} %get-tuple-element.3, bf16[192,2048]{1,0:T(8,128)(2,1)S(1)} %multiply_convert_fusion.1, s32[1024]{0:T(1024)S(1)} %pad_clamp_fusion.1, bf16[]{:T(256)} %constant.35.clone.1), kind=kCustom, calls=%fused_computation.11 | custom fusion | bytes 2097154 | tf_op jit(solution)/shard_map/scatter | solution.py:54
  25.0 64.1 %all_to_all.10 = bf16[64,8,2048]{2,1,0:T(8,128)(2,1)} all-to-all(bf16[64,8,2048]{2,1,0:T(8,128)(2,1)S(1)} %bitcast.71), channel_id=1, replica_groups=mesh['grp'=4,'dev'=64] {'dev'}, dimensions={0} | all-to-all | bytes 4194304 | tf_op jit(solution)/shard_map/all_to_all | solution.py:59
  89.1 10.5 %fusion.1 = f32[64,8,2048]{2,1,0:T(8,128)} fusion(bf16[1,1024,2048]{2,1,0:T(8,128)(2,1)} %param.18, bf16[1,2048,1024]{2,1,0:T(8,128)(2,1)} %param.17, bf16[64,8,2048]{2,1,0:T(8,128)(2,1)} %all_to_all.10), kind=kOutput, calls=%fused_computation.4 | convolution fusion | flops 4296015872 | bytes 14680064 | tf_op jit(solution)/shard_map/dot_general | solution.py:64
  99.6 6.1 %all-to-all-start.1 = ((f32[64,8,2048]{2,1,0:T(8,128)}), f32[64,8,2048]{2,1,0:T(8,128)}, u32[]{:S(2)}, u32[]{:S(2)}) async-start(f32[64,8,2048]{2,1,0:T(8,128)} %fusion.1), calls=%async_computation.1 | async-start | bytes 8388608 | tf_op jit(solution)/shard_map/all_to_all | solution.py:65
  106.1 95.6 %all-to-all-done.1 = f32[64,8,2048]{2,1,0:T(8,128)} async-done(((f32[64,8,2048]{2,1,0:T(8,128)}), f32[64,8,2048]{2,1,0:T(8,128)}, u32[]{:S(2)}, u32[]{:S(2)}) %all-to-all-start.1) | async-done | bytes 4194336 | tf_op jit(solution)/shard_map/all_to_all | solution.py:65
  201.7 6.5 %gather_fusion = f32[384,2048]{1,0:T(8,128)S(1)} fusion(f32[512,2048]{1,0:T(8,128)} %bitcast.8, s32[1024]{0:T(1024)S(1)} %pad_clamp_fusion), kind=kCustom, calls=%fused_computation.1 | custom fusion | bytes 6292992 | tf_op jit(solution)/shard_map/gather | solution.py:74
  208.2 3.2 gather.10
  211.4 8.0 %multiply_reduce_fusion = f32[192,2048]{1,0:T(8,128)} fusion(f32[192,2,2048]{2,1,0:T(2,128)} %gather.10, f32[192,2]{1,0:T(8,128)S(1)} %copy.28), kind=kLoop, calls=%fused_computation.8 | loop fusion | flops 1179648 | bytes 4720128 | tf_op jit(solution)/shard_map/reduce_sum | solution.py:75
  219.5 0.5 all-gather.3.cloned.1.call-update
  220.1 0.5 all-gather.5.cloned.1.call-update
  220.7 51.0 %all-reduce.2.cloned.1.call-done = f32[192,2048]{1,0:T(8,128)} async-done(((f32[192,2048]{1,0:T(8,128)}), f32[192,2048]{1,0:T(8,128)}) %all-reduce.2.cloned.1.call-update) | async-done | bytes 1572880 | tf_op jit(solution)/shard_map/psum | solution.py:75
  271.7 1.7 fusion.45
  273.4 0.3 multiply_reduce_fusion.1
  273.7 0.3 multiply_convert_fusion
  274.1 23.3 %all-gather.3.cloned.1.call-done = bf16[2048,512]{1,0:T(8,128)(2,1)} async-done(((bf16[32,512]{1,0:T(8,128)(2,1)}), bf16[2048,512]{1,0:T(8,128)(2,1)}) %all-gather.3.cloned.1.call-update) | async-done | bytes 2097168 | tf_op jit(solution)/shard_map/all_gather | solution.py:78
  297.3 2.2 convolution_convert_fusion.1
  299.5 75.5 %all-gather.5.cloned.1.call-done = bf16[2048,512]{1,0:T(8,128)(2,1)} async-done(((bf16[32,512]{1,0:T(8,128)(2,1)}), bf16[2048,512]{1,0:T(8,128)(2,1)}) %all-gather.5.cloned.1.call-update) | async-done | bytes 2097168 | tf_op jit(solution)/shard_map/all_gather | solution.py:79
  375.1 2.2 convolution_convert_fusion
  377.3 0.2 fusion.27
  377.6 0.2 fusion.25
  377.8 0.6 copy.45
  (48 shorter events, 1.9 us)
Async XLA Ops:
  8.0 8.1 %copy-start = (bf16[2,96,2048]{2,1,0:T(8,128)(2,1)S(1)}, bf16[2,96,2048]{2,1,0:T(8,128)(2,1)}, u32[]{:S(2)}) copy-start(bf16[2,96,2048]{2,1,0:T(8,128)(2,1)} %param.11) | copy-start | bytes 2359300
  8.0 8.1 %copy-start.3 = (f32[2048]{0:T(1024)S(1)}, f32[2048]{0:T(1024)}, u32[]{:S(2)}) copy-start(f32[2048]{0:T(1024)} %param.12) | copy-start | bytes 24580
  99.6 6.2 %copy-start.6 = (f32[2,96,2]{1,2,0:T(2,128)S(1)}, f32[2,96,2]{1,2,0:T(2,128)}, u32[]{:S(2)}) copy-start(f32[2,96,2]{1,2,0:T(2,128)} %param.15) | copy-start | bytes 4612
  99.6 102.0 %all-to-all-start.1 = ((f32[64,8,2048]{2,1,0:T(8,128)}), f32[64,8,2048]{2,1,0:T(8,128)}, u32[]{:S(2)}, u32[]{:S(2)}) async-start(f32[64,8,2048]{2,1,0:T(8,128)} %fusion.1), calls=%async_computation.1 | async-start | bytes 8388608 | tf_op jit(solution)/shard_map/all_to_all | solution.py:65
  105.8 165.9 %all-reduce.2.cloned.1.call-start = ((), (), s32[]{:S(2)}) async-start(), calls=%async_computation.2 | async-start | bytes 3145728 | tf_op jit(solution)/shard_map/psum | solution.py:75
  211.4 9.2 %copy-start.5 = (bf16[2,512]{1,0:T(2,128)(2,1)S(1)}, bf16[2,512]{1,0:T(2,128)(2,1)}, u32[]{:S(2)}) copy-start(bf16[2,512]{1,0:T(2,128)(2,1)} %param.21) | copy-start | bytes 6148
  211.4 60.3 %copy-start.1 = (bf16[2,96,2048]{2,1,0:T(8,128)(2,1)S(1)}, bf16[2,96,2048]{2,1,0:T(8,128)(2,1)}, u32[]{:S(2)}) copy-start(bf16[2,96,2048]{2,1,0:T(8,128)(2,1)} %param.11) | copy-start | bytes 2359300
  219.5 77.8 %all-gather.3.cloned.1.call-start = ((), (), s32[]{:S(2)}) async-start(), calls=%async_computation.3 | async-start | bytes 2129920 | tf_op jit(solution)/shard_map/all_gather | solution.py:78
  220.1 155.0 %all-gather.5.cloned.1.call-start = ((), (), s32[]{:S(2)}) async-start(), calls=%async_computation.4 | async-start | bytes 2129920 | tf_op jit(solution)/shard_map/all_gather | solution.py:79
  271.7 2.0 copy-start.4
  274.0 103.2 %copy-start.2 = (bf16[192,2048]{1,0:T(8,128)(2,1)}, bf16[192,2048]{1,0:T(8,128)(2,1)S(1)}, u32[]{:S(2)}) copy-start(bf16[192,2048]{1,0:T(8,128)(2,1)S(1)} %multiply_convert_fusion) | copy-start | bytes 2359300
Sparse Core Ops, SparseCore 0:
  219.6 52.0 all-reduce.1
Sparse Core Ops, SparseCore 1:
  222.7 74.5 all-gather.2
  300.0 75.0 all-gather.4
where the time goes:
time: 386 us
  waiting for transfers between devices  246 us (64%)
  blocking collectives  64.1 us (17%)
  local copies, waits for them, and re-layouts  21.7 us (6%)
  other arithmetic  16.3 us (4%)
  between operations  15.7 us (4%)
  matrix products  15.2 us (4%)
  starting transfers between devices  6.26 us (2%)
    all_to_all x1, waiting for transfers between devices, on_device(): lax.all_to_all(outputs.reshape(arrived.shape[0], arrived.shape[1], model_...  95.6 us
    all_gather x1, waiting for transfers between devices, on_device(): value_rows = lax.all_gather(w_value, 'dev', axis=0, tiled=True)  75.5 us
    all_to_all x1, blocking collectives, on_device(): lax.all_to_all(dispatch_buffer, 'dev', split_axis=0, concat_axis=0, tiled...  64.1 us
    psum x1, waiting for transfers between devices, on_device(): lax.psum(jnp.sum(picked.reshape(row_count, 2, feature_count), axis=1), 'g...  51 us
    all_gather x1, waiting for transfers between devices, on_device(): key_rows = lax.all_gather(w_key, 'dev', axis=0, tiled=True)  23.3 us
    dot_general x1, matrix products, on_device(): outputs = jnp.dot(hidden, w_out[0], preferred_element_type=jnp.float32)  10.5 us
    gather x2, local copies, waits for them, and re-layouts, on_device(): picked = flat_back[safe_target] * gate_pairs[:, None]  9.75 us
    scatter x1, local copies, waits for them, and re-layouts, on_device(): dispatch_buffer = jnp.zeros((experts * capacity, model_width), jnp.bfloat...  8.48 us
  transfers between devices with their start and end apart: 4, of which 4 were waited for; matrix products, arithmetic and copies ran while one was open for 1% of the time, Pallas kernels for 0%

commit v1 on v0

v1 whole, which is shorter than its diff:
```python
import functools
import math

import jax
import jax.numpy as jnp
from jax import lax
from jax.experimental import pallas as pl
from jax.experimental.pallas import tpu as pltpu
from jax.sharding import PartitionSpec as P

HEADS = 16
CAPACITY = 8
EPSILON = 1e-05
F32 = jnp.float32
BF16 = jnp.bfloat16
MESH = pl.DeviceIdType.MESH


def moe_kernel(
    n_exp,
    n_x,
    enc_ref,
    ngain_ref,
    fgain_ref,
    ids_ref,
    gates_ref,
    lens_ref,
    win_hbm,
    wout_hbm,
    out_ref,
    win,
    wout,
    normed,
    dispatch,
    xbuf,
    combine,
    xrow,
    hid,
    part,
    st1,
    rv1,
    st2,
    rv2,
    back,
    ybuf,
    mix,
    w_sem,
    a2a_send,
    a2a_recv,
    yag_send,
    yag_recv,
    rs_send,
    rs_recv,
    ret_send,
    ret_recv,
    mix_send,
    mix_recv,
):
    rows, width = enc_ref.shape
    sent = lens_ref.shape[0]
    length = rows // sent
    quarter = width // 4
    half = quarter // 2
    per = n_exp // n_x
    crow = per * CAPACITY
    mrow = per * 2 * CAPACITY
    prow = normed.shape[0]

    g = lax.axis_index("grp")
    d = lax.axis_index("dev")
    my_x = d // per
    my_z = d % per
    right, left, diag = (g + 1) % 4, (g + 3) % 4, (g + 2) % 4

    load_in = pltpu.make_async_copy(win_hbm, win, w_sem.at[0])
    load_out = pltpu.make_async_copy(wout_hbm, wout, w_sem.at[1])
    load_in.start()
    load_out.start()

    barrier = pltpu.get_barrier_semaphore()

    def greet(i, carry):
        pl.semaphore_signal(barrier, inc=1, device_id=(g, (d + i) % n_exp), device_id_type=MESH)
        return carry

    lax.fori_loop(1, n_exp, greet, 0)
    for i in range(1, 4):
        pl.semaphore_signal(barrier, inc=1, device_id=((g + i) % 4, d), device_id_type=MESH)

    blk = 16
    qcols = pl.ds(pl.multiple_of(g * quarter, 128), quarter)

    def norm_block(i, carry):
        r = pl.ds(pl.multiple_of(i * blk, blk), blk)
        v = enc_ref[r, :].astype(F32)
        mean = jnp.mean(v, axis=-1, keepdims=True)
        c = v - mean
        var = jnp.mean(c * c, axis=-1, keepdims=True)
        own = enc_ref[r, qcols].astype(F32) - mean
        own = own * lax.rsqrt(var + EPSILON) * ngain_ref[:, qcols]
        normed[r, :] = own.astype(BF16)
        return carry

    lax.fori_loop(0, rows // blk, norm_block, 0)
    if prow > rows:
        normed[rows:, :] = jnp.zeros((prow - rows, quarter), BF16)

    pos = lax.broadcasted_iota(jnp.int32, (rows, 1), 0)
    live = jnp.zeros((rows, 1), jnp.bool_)
    for s in range(sent):
        live = live | ((pos >= s * length) & (pos < s * length + lens_ref[s]))
    lane = lax.broadcasted_iota(jnp.int32, (rows, 128), 1)
    earlier = (
        lax.broadcasted_iota(jnp.int32, (rows, rows), 0)
        > lax.broadcasted_iota(jnp.int32, (rows, rows), 1)
    ).astype(BF16)
    codes = []
    offset = jnp.zeros((1, 128), F32)
    for k in range(2):
        hot = jnp.where((ids_ref[:, k : k + 1] == lane) & live, 1.0, 0.0).astype(F32)
        rank = jnp.dot(earlier, hot.astype(BF16), preferred_element_type=F32) + offset
        offset = offset + jnp.sum(hot, axis=0, keepdims=True)
        code = jnp.sum(
            hot * (rank + (2 * CAPACITY) * lane.astype(F32)), axis=1, keepdims=True
        )
        codes.append(jnp.where(live, code, -100.0))
    cols = jnp.where(lane == 0, codes[0], jnp.where(lane == 1, codes[1], -100.0))
    if prow > rows:
        cols = jnp.concatenate([cols, jnp.full((prow - rows, 128), -100.0, F32)], axis=0)
    trow = cols.T.astype(jnp.int32)
    row0, row1 = trow[0:1, :], trow[1:2, :]
    code0, code1 = codes[0].astype(jnp.int32), codes[1].astype(jnp.int32)
    gate0, gate1 = gates_ref[:, 0:1], gates_ref[:, 1:2]

    pl.semaphore_wait(barrier, n_exp - 1 + 3)

    for c in range(n_x):
        base = ((my_x + c) % n_x) * mrow
        r = lax.broadcasted_iota(jnp.int32, (mrow, prow), 0) + base
        acc = jnp.zeros((mrow, half), F32)
        for h in range(2):
            rh = r - h * CAPACITY
            pick = jnp.where((rh == row0) | (rh == row1), 1.0, 0.0).astype(BF16)
            acc = acc + jnp.dot(
                pick, normed[:, h * half : (h + 1) * half], preferred_element_type=F32
            )
        dispatch[c] = acc.astype(BF16).reshape(per, 2 * CAPACITY, half)

        def send(j, carry, c=c):
            z = (my_z + j) % per
            pltpu.make_async_remote_copy(
                src_ref=dispatch.at[c, z],
                dst_ref=xbuf.at[g, d],
                send_sem=a2a_send.at[c],
                recv_sem=a2a_recv.at[c],
                device_id=(g, ((my_x + c) % n_x) * per + z),
                device_id_type=MESH,
            ).start()
            return carry

        if c == 0:
            pltpu.make_async_copy(
                dispatch.at[0, my_z], xbuf.at[g, d], a2a_recv.at[0]
            ).start()
            lax.fori_loop(1, per, send, 0)
        else:
            lax.fori_loop(0, per, send, 0)

    for c in range(n_x):
        base = ((my_x + c) % n_x) * mrow
        col = lax.broadcasted_iota(jnp.int32, (rows, mrow), 1) + base
        for h in range(2):
            ch = col - h * CAPACITY
            value = jnp.where(ch == code0, gate0, jnp.where(ch == code1, gate1, 0.0))
            high = value.astype(BF16)
            combine[c, 2 * h * rows : (2 * h + 1) * rows, :] = high
            combine[c, (2 * h + 1) * rows : (2 * h + 2) * rows, :] = (
                value - high.astype(F32)
            ).astype(BF16)

    def slab(c):
        return ((my_x + n_x - c) % n_x) * per

    def ycopy(src, dst, send_sem, recv_sem, to):
        return pltpu.make_async_remote_copy(
            src_ref=src,
            dst_ref=dst,
            send_sem=send_sem,
            recv_sem=recv_sem,
            device_id=(to, d),
            device_id_type=MESH,
        )

    def xs(q, c, start=0, size=per):
        return xbuf.at[q, pl.ds(slab(c) + start, size)]

    def arrived(ref, sem):
        pltpu.make_async_copy(ref, ref, sem).wait()

    hp = per // 2
    sends = []

    def stage_a(c):
        arrived(xs(g, c), a2a_recv.at[c])
        for i, to in enumerate((right, left)):
            cp = ycopy(xs(g, c), xs(g, c), yag_send.at[c, i], yag_recv.at[c, i], to)
            cp.start()
            sends.append(cp)

    def stage_b(c):
        arrived(xs(left, c), yag_recv.at[c, 0])
        cp = ycopy(
            xs(left, c, 0, hp), xs(left, c, 0, hp), yag_send.at[c, 2], yag_recv.at[c, 2], right
        )
        cp.start()
        sends.append(cp)
        arrived(xs(right, c), yag_recv.at[c, 1])
        cp = ycopy(
            xs(right, c, hp, hp), xs(right, c, hp, hp), yag_send.at[c, 3], yag_recv.at[c, 3], left
        )
        cp.start()
        sends.append(cp)

    hrow = crow // 2

    def stage_c(c):
        arrived(xs(diag, c, 0, hp), yag_recv.at[c, 2])
        arrived(xs(diag, c, hp, hp), yag_recv.at[c, 3])
        for q in range(4):
            block = xbuf[q, pl.ds(slab(c), per)].astype(F32)
            for h in range(2):
                xrow[:, q * quarter + h * half : q * quarter + (h + 1) * half] = (
                    block[:, h * CAPACITY : (h + 1) * CAPACITY, :]
                    .reshape(crow, half)
                    .astype(BF16)
                )
        if c == 0:
            load_in.wait()
        tile = min(256, hid.shape[1])

        def first(n, carry):
            cs = pl.ds(pl.multiple_of(n * tile, tile), tile)
            hid[:, cs] = jnp.maximum(
                jnp.dot(xrow[...], win[:, cs], preferred_element_type=F32), 0.0
            ).astype(BF16)
            return carry

        lax.fori_loop(0, hid.shape[1] // tile, first, 0)
        if c == 0:
            load_out.wait()

        def second(q):
            cs = pl.ds(pl.multiple_of(q * quarter, 128), quarter)
            return jnp.dot(hid[...], wout[:, cs], preferred_element_type=F32)

        st1[c] = second(diag).astype(BF16)
        for i, to in enumerate((right, left)):
            cp = ycopy(
                st1.at[c, pl.ds(i * hrow, hrow)],
                rv1.at[c, pl.ds(i * hrow, hrow)],
                rs_send.at[c, i],
                rs_recv.at[c, i],
                to,
            )
            cp.start()
            sends.append(cp)

        part[c, 0] = second(right)
        part[c, 1] = second(left)
        part[c, 2] = second(g)

    def stage_d(c):
        for i, to in enumerate((right, left)):
            a, b = i * hrow, (1 - i) * hrow
            arrived(rv1.at[c, pl.ds(a, hrow)], rs_recv.at[c, i])
            st2[c, i, a : a + hrow, :] = (
                part[c, i, a : a + hrow, :] + rv1[c, a : a + hrow, :].astype(F32)
            ).astype(BF16)
            st2[c, i, b : b + hrow, :] = part[c, i, b : b + hrow, :].astype(BF16)
            cp = ycopy(st2.at[c, i], rv2.at[c, i], rs_send.at[c, 2 + i], rs_recv.at[c, 2 + i], to)
            cp.start()
            sends.append(cp)

    def stage_e(c):
        for i in range(2):
            arrived(rv2.at[c, i], rs_recv.at[c, 2 + i])
        total = part[c, 2] + rv2[c, 0].astype(F32) + rv2[c, 1].astype(F32)
        total = total.reshape(per, CAPACITY, quarter)
        back[c] = jnp.concatenate([total[:, :, :half], total[:, :, half:]], axis=1).astype(BF16)

        def send(j, carry):
            z = (my_z + j) % per
            pltpu.make_async_remote_copy(
                src_ref=back.at[c, z],
                dst_ref=ybuf.at[d],
                send_sem=ret_send.at[c],
                recv_sem=ret_recv.at[c],
                device_id=(g, slab(c) + z),
                device_id_type=MESH,
            ).start()
            return carry

        if c == 0:
            pltpu.make_async_copy(back.at[0, my_z], ybuf.at[d], ret_recv.at[0]).start()
            lax.fori_loop(1, per, send, 0)
        else:
            lax.fori_loop(0, per, send, 0)

    stages = (stage_a, stage_b, stage_c, stage_d, stage_e)
    for step in range(n_x + len(stages) - 1):
        for k in reversed(range(len(stages))):
            if 0 <= step - k < n_x:
                stages[k](step - k)

    acc = jnp.zeros((4 * rows, half), F32)
    for c in range(n_x):
        here = pl.ds(((my_x + c) % n_x) * per, per)
        arrived(ybuf.at[here], ret_recv.at[c])
        acc = acc + jnp.dot(
            combine[c], ybuf[here].reshape(mrow, half), preferred_element_type=F32
        )
    mix[g] = jnp.concatenate(
        [acc[:rows] + acc[rows : 2 * rows], acc[2 * rows : 3 * rows] + acc[3 * rows :]], axis=1
    ).astype(BF16)

    hm = rows // 2
    for i, to in enumerate((right, left)):
        cp = ycopy(mix.at[g], mix.at[g], mix_send.at[i], mix_recv.at[i], to)
        cp.start()
        sends.append(cp)
    for i, (origin, to) in enumerate(((left, right), (right, left))):
        arrived(mix.at[origin], mix_recv.at[i])
        piece = mix.at[origin, pl.ds(i * hm, hm)]
        cp = ycopy(piece, piece, mix_send.at[2 + i], mix_recv.at[2 + i], to)
        cp.start()
        sends.append(cp)
    for i in range(2):
        arrived(mix.at[diag, pl.ds(i * hm, hm)], mix_recv.at[2 + i])

    def final_block(i, carry):
        r = pl.ds(pl.multiple_of(i * blk, blk), blk)
        m = jnp.concatenate([mix[q, r, :] for q in range(4)], axis=1)
        v = enc_ref[r, :].astype(F32) + m.astype(F32)
        mean = jnp.mean(v, axis=-1, keepdims=True)
        cen = v - mean
        var = jnp.mean(cen * cen, axis=-1, keepdims=True)
        out_ref[r, :] = (cen * lax.rsqrt(var + EPSILON) * fgain_ref[...]).astype(BF16)
        return carry

    lax.fori_loop(0, rows // blk, final_block, 0)

    for cp in sends:
        cp.wait_send()
    for c in range(n_x):
        count = per - 1 if c == 0 else per
        for buf, sem in ((dispatch, a2a_send), (back, ret_send)):
            arrived(buf.at[c, pl.ds(0, count)], sem.at[c])


def experts_layer(n_exp, enc, ngain, fgain, ids, gates, lens, w_in, w_out):
    rows, width = enc.shape
    n_x = 4 if n_exp >= 16 else 2
    per = n_exp // n_x
    quarter, half = width // 4, width // 8
    crow, mrow = per * CAPACITY, per * 2 * CAPACITY
    ff = w_in.shape[1]
    prow = -(-rows // 128) * 128
    vmem = pl.BlockSpec(memory_space=pltpu.VMEM)
    hbm = pl.BlockSpec(memory_space=pl.ANY)
    smem = pl.BlockSpec(memory_space=pltpu.SMEM)
    dma = pltpu.SemaphoreType.DMA
    return pl.pallas_call(
        functools.partial(moe_kernel, n_exp, n_x),
        out_shape=jax.ShapeDtypeStruct((rows, width), BF16),
        in_specs=[vmem, vmem, vmem, vmem, vmem, smem, hbm, hbm],
        out_specs=vmem,
        scratch_shapes=[
            pltpu.VMEM(w_in.shape, BF16),
            pltpu.VMEM(w_out.shape, BF16),
            pltpu.VMEM((prow, quarter), BF16),
            pltpu.VMEM((n_x, per, 2 * CAPACITY, half), BF16),
            pltpu.VMEM((4, n_exp, 2 * CAPACITY, half), BF16),
            pltpu.VMEM((n_x, 4 * rows, mrow), BF16),
            pltpu.VMEM((crow, width), BF16),
            pltpu.VMEM((crow, ff), BF16),
            pltpu.VMEM((n_x, 3, crow, quarter), F32),
            pltpu.VMEM((n_x, crow, quarter), BF16),
            pltpu.VMEM((n_x, crow, quarter), BF16),
            pltpu.VMEM((n_x, 2, crow, quarter), BF16),
            pltpu.VMEM((n_x, 2, crow, quarter), BF16),
            pltpu.VMEM((n_x, per, 2 * CAPACITY, half), BF16),
            pltpu.VMEM((n_exp, 2 * CAPACITY, half), BF16),
            pltpu.VMEM((4, rows, quarter), BF16),
            dma((2,)),
            dma((n_x,)),
            dma((n_x,)),
            dma((n_x, 4)),
            dma((n_x, 4)),
            dma((n_x, 4)),
            dma((n_x, 4)),
            dma((n_x,)),
            dma((n_x,)),
            dma((4,)),
            dma((4,)),
        ],
        compiler_params=pltpu.CompilerParams(
            collective_id=0, has_side_effects=True, vmem_limit_bytes=48 * 1024 * 1024
        ),
        cost_estimate=pl.CostEstimate(
            flops=4 * n_exp * CAPACITY * width * ff,
            bytes_accessed=200_000_000,
            transcendentals=0,
        ),
    )(enc, ngain, fgain, ids, gates, lens, w_in, w_out)


def on_device(
    n_exp,
    enc_states,
    norm_gain,
    final_gain,
    expert_ids,
    expert_gates,
    source_lengths,
    w_in,
    w_out,
    w_key,
    w_value,
    cross_query,
):
    sentences, length, model_width = enc_states.shape
    row_count = sentences * length
    key_rows = lax.all_gather(w_key, "dev", axis=0, tiled=True)
    value_rows = lax.all_gather(w_value, "dev", axis=0, tiled=True)
    encoded = experts_layer(
        n_exp,
        enc_states.reshape(row_count, model_width),
        norm_gain.reshape(1, model_width),
        final_gain.reshape(1, model_width),
        expert_ids.reshape(row_count, 2),
        expert_gates.reshape(row_count, 2),
        source_lengths,
        w_in[0],
        w_out[0],
    )
    positions = lax.broadcasted_iota(jnp.int32, (sentences, length), 1)
    live_mask = positions < source_lengths[:, None]
    column_count = w_key.shape[1]
    key_sum = jnp.dot(encoded, key_rows, preferred_element_type=jnp.float32)
    value_sum = jnp.dot(encoded, value_rows, preferred_element_type=jnp.float32)
    head_dim = model_width // HEADS
    local_heads = column_count // head_dim
    key_cache = key_sum.astype(jnp.bfloat16).reshape(sentences, length, local_heads, head_dim)
    value_cache = value_sum.astype(jnp.bfloat16).reshape(sentences, length, local_heads, head_dim)
    queries = cross_query.reshape(sentences, local_heads, head_dim)
    scores = jnp.einsum("shd,sthd->sht", queries, key_cache, preferred_element_type=jnp.float32) * (
        1.0 / math.sqrt(head_dim)
    )
    weights = jnp.exp(scores) * live_mask[:, None, :].astype(jnp.float32)
    probabilities = (weights / jnp.sum(weights, axis=-1, keepdims=True)).astype(jnp.bfloat16)
    context = jnp.einsum(
        "sht,sthd->shd", probabilities, value_cache, preferred_element_type=jnp.float32
    )
    return (
        encoded.reshape(sentences, length, model_width),
        context.astype(jnp.bfloat16).reshape(sentences, column_count),
    )


def solution(mesh):
    return jax.shard_map(
        functools.partial(on_device, mesh.shape["dev"]),
        mesh=mesh,
        in_specs=(
            P("dev", None, None),
            P(),
            P(),
            P("dev", None, None),
            P("dev", None, None),
            P("dev"),
            P("dev", None, "grp"),
            P("dev", "grp", None),
            P("dev", "grp"),
            P("dev", "grp"),
            P("dev", "grp"),
        ),
        out_specs=(P("dev", None, None), P("dev", "grp")),
        check_vma=False,
    )
```

time: 386 us -> 183 us (0.47)
  waiting for transfers between devices: 246 us -> 70.2 us
  Pallas kernels: 0 us -> 83.7 us
  blocking collectives: 64.1 us -> 0 us
  other arithmetic: 16.3 us -> 0.17 us
  local copies, waits for them, and re-layouts: 21.7 us -> 9.23 us
  matrix products: 15.2 us -> 4.71 us
  starting transfers between devices: 6.26 us -> 0.08 us
    all_to_all x1 -> x0, waiting for transfers between devices: 95.6 us -> none  [on_device(): lax.all_to_all(outputs.reshape(arrived.shape[0], arrived.shape[1], model_...]
    pallas_call x0 -> x1, Pallas kernels: none -> 83.7 us  [experts_layer(): pl.pallas_call(functools.partial(moe_kernel, n_exp, n_x), out_shape=jax.S...]
    all_to_all x1 -> x0, blocking collectives: 64.1 us -> none  [on_device(): lax.all_to_all(dispatch_buffer, 'dev', split_axis=0, concat_axis=0, tiled...]
    psum x1 -> x0, waiting for transfers between devices: 51 us -> none  [on_device(): lax.psum(jnp.sum(picked.reshape(row_count, 2, feature_count), axis=1), 'g...]
    all_gather x1, waiting for transfers between devices: 23.3 us -> 0.01 us  [on_device(): key_rows = lax.all_gather(w_key, 'dev', axis=0, tiled=True)]
    reduce_sum x6 -> x0, other arithmetic: 12.9 us -> none  [the longest x1 8.04 us: on_device(): jnp.sum(picked.reshape(row_count, 2, feature_count), axis=1)]
    dot_general x1 -> x0, matrix products: 10.5 us -> none  [on_device(): outputs = jnp.dot(hidden, w_out[0], preferred_element_type=jnp.float32)]
    gather x2 -> x0, local copies, waits for them, and re-layouts: 9.75 us -> none  [on_device(): picked = flat_back[safe_target] * gate_pairs[:, None]]
  transfers between devices with their start and end apart: 4 -> 2, of which waited for: 4 -> 1; matrix products, arithmetic and copies ran while one was open for 1% -> 3% of each run, Pallas kernels for 0% -> 46%
where the time goes in v1:
time: 183 us; the launch traced here: 182 us
  Pallas kernels  83.7 us (46%)
  waiting for transfers between devices  70.2 us (38%)
  between operations  14.1 us (8%)
  local copies, waits for them, and re-layouts  9.23 us (5%)
  matrix products  4.71 us (3%)
    pallas_call x1, Pallas kernels, experts_layer(): pl.pallas_call(functools.partial(moe_kernel, n_exp, n_x), out_shape=jax.S...  83.7 us
    all_gather x1, waiting for transfers between devices, on_device(): value_rows = lax.all_gather(w_value, 'dev', axis=0, tiled=True)  68.9 us
    unnamed x14, local copies, waits for them, and re-layouts  8.43 us
  transfers between devices with their start and end apart: 2, of which 1 were waited for; matrix products, arithmetic and copies ran while one was open for 3% of the time, Pallas kernels for 46%

profile of v1, /device:TPU:1, one launch (start us, length us, event | category | flops | bytes accessed | tf_op | source)
XLA Modules:
  0.0 182.3 jit_solution(7397461686890575524)
XLA Ops:
  7.2 0.0 all-gather.3.cloned.1.call-start
  7.2 0.7 all-gather.3.cloned.1.call-update
  7.9 0.0 all-gather.5.cloned.1.call-start
  7.9 0.7 all-gather.5.cloned.1.call-update
  8.6 0.8 copy.15
  9.4 0.8 copy.16
  10.3 0.7 reshape.67
  10.9 0.0 copy-start
  10.9 2.2 %copy-done = bf16[1,2048,1024]{2,1,0:T(8,128)(2,1)S(1)} copy-done((bf16[1,2048,1024]{2,1,0:T(8,128)(2,1)S(1)}, bf16[1,2048,1024]{2,1,0:T(8,128)(2,1)}, u32[]{:S(2)}) %copy-start) | copy-done | bytes 4194328
  13.1 0.0 copy-start.1
  13.1 1.1 copy-done.1
  14.3 0.0 copy-start.2
  14.3 0.7 copy-done.2
  15.0 0.0 copy-start.3
  15.0 0.7 copy-done.3
  15.7 0.0 copy-start.4
  15.7 0.7 copy-done.4
  16.3 83.7 %shard_map.122 = bf16[192,2048]{1,0:T(8,128)(2,1)S(1)} custom-call(bf16[192,2048]{1,0:T(8,128)(2,1)S(1)} %bitcast.28, f32[1,2048]{1,0:T(1,128)S(1)} %bitcast.29, f32[1,2048]{1,0:T(1,128)S(1)} %bitcast.30, s32[192,2]{1,0:T(8,128)S(1)} %bitcast.25, f32[192,2]{1,0:T(8,128)S(1)} %bitcast.26, s32[2]{0:T(128)S(1)} %copy-done.4, bf16[2048,1024]{1,0:T(8,128)(2,1)S(1)} %bitcast.27, ...), custom_call_target="tpu_custom_call" | custom-call | flops 4294967296 | bytes 200000000 | tf_op jit(solution)/shard_map/pallas_call | solution.py:372
  100.1 0.1 compare_convert_fusion
  100.1 0.0 all-gather.3.cloned.1.call-done
  100.1 2.2 %convolution_convert_fusion.1 = bf16[192,512]{1,0:T(8,128)(2,1)S(1)} fusion(bf16[192,2048]{1,0:T(8,128)(2,1)S(1)} %shard_map.122, bf16[2048,512]{1,0:T(8,128)(2,1)} %all-gather.3.cloned.1.call-done), kind=kOutput, calls=%fused_computation.2 | convolution fusion | flops 402751488 | bytes 3080192 | tf_op jit(solution)/shard_map/dot_general | solution.py:449
  102.3 0.1 reshape.58
  102.4 68.9 %all-gather.5.cloned.1.call-done = bf16[2048,512]{1,0:T(8,128)(2,1)} async-done(((bf16[32,512]{1,0:T(8,128)(2,1)}), bf16[2048,512]{1,0:T(8,128)(2,1)}) %all-gather.5.cloned.1.call-update) | async-done | bytes 2097168 | tf_op jit(solution)/shard_map/all_gather | solution.py:434
  171.2 2.2 %convolution_convert_fusion = bf16[192,512]{1,0:T(8,128)(2,1)S(1)} fusion(bf16[192,2048]{1,0:T(8,128)(2,1)S(1)} %shard_map.122, bf16[2048,512]{1,0:T(8,128)(2,1)} %all-gather.5.cloned.1.call-done), kind=kOutput, calls=%fused_computation.1 | convolution fusion | flops 402751488 | bytes 3080192 | tf_op jit(solution)/shard_map/dot_general | solution.py:450
  173.4 0.1 reshape.60
  173.5 0.2 fusion.6
  173.7 0.1 fusion.3
  173.7 0.2 fusion.4
  173.9 0.6 copy.31
  174.5 0.9 copy.33
  (1 shorter events, 0.0 us)
Async XLA Ops:
  7.2 93.0 %all-gather.3.cloned.1.call-start = ((), (), s32[]{:S(2)}) async-start(), calls=%async_computation | async-start | bytes 2129920 | tf_op jit(solution)/shard_map/all_gather | solution.py:433
  7.9 163.3 %all-gather.5.cloned.1.call-start = ((), (), s32[]{:S(2)}) async-start(), calls=%async_computation.1 | async-start | bytes 2129920 | tf_op jit(solution)/shard_map/all_gather | solution.py:434
  10.9 2.2 %copy-start = (bf16[1,2048,1024]{2,1,0:T(8,128)(2,1)S(1)}, bf16[1,2048,1024]{2,1,0:T(8,128)(2,1)}, u32[]{:S(2)}) copy-start(bf16[1,2048,1024]{2,1,0:T(8,128)(2,1)} %param.17) | copy-start | bytes 12582916
  13.1 1.1 copy-start.1
  14.3 0.7 copy-start.2
  15.0 0.7 copy-start.3
  15.7 0.7 copy-start.4
Sparse Core Ops, SparseCore 0:
  10.8 82.6 all-gather.2
  96.3 74.9 all-gather.4

commit v2 on v1

--- a/solution.py
+++ b/solution.py
@@ -9,6 +9,7 @@
 from jax.sharding import PartitionSpec as P
 
 HEADS = 16
+HEAD_DIM = 128
 CAPACITY = 8
 EPSILON = 1e-05
 F32 = jnp.float32
@@ -16,20 +17,29 @@
 MESH = pl.DeviceIdType.MESH
 
 
-def moe_kernel(
+def layer_kernel(
     n_exp,
     n_x,
+    lens_ref,
+    ids_ref,
+    gates_ref,
+    query_ref,
+    enc_hbm,
+    ngain_hbm,
+    fgain_hbm,
+    wkey_hbm,
+    wvalue_hbm,
+    win_hbm,
+    wout_hbm,
+    out_ref,
+    context_ref,
     enc_ref,
     ngain_ref,
     fgain_ref,
-    ids_ref,
-    gates_ref,
-    lens_ref,
-    win_hbm,
-    wout_hbm,
-    out_ref,
+    wkv,
     win,
     wout,
+    qkey,
     normed,
     dispatch,
     xbuf,
@@ -55,10 +65,15 @@
     ret_recv,
     mix_send,
     mix_recv,
+    kvx_send,
+    kvx_recv,
+    kvz_send,
+    kvz_recv,
+    kvc_send,
+    kvc_recv,
 ):
     rows, width = enc_ref.shape
-    sent = lens_ref.shape[0]
-    length = rows // sent
+    sent, _, length = ids_ref.shape
     quarter = width // 4
     half = quarter // 2
     per = n_exp // n_x
@@ -72,10 +87,22 @@
     my_z = d % per
     right, left, diag = (g + 1) % 4, (g + 3) % 4, (g + 2) % 4
 
-    load_in = pltpu.make_async_copy(win_hbm, win, w_sem.at[0])
-    load_out = pltpu.make_async_copy(wout_hbm, wout, w_sem.at[1])
-    load_in.start()
-    load_out.start()
+    loads = [
+        pltpu.make_async_copy(src, dst, w_sem.at[i])
+        for i, (src, dst) in enumerate(
+            (
+                (enc_hbm, enc_ref),
+                (ngain_hbm, ngain_ref),
+                (wkey_hbm, wkv.at[my_x, my_z, 0]),
+                (wvalue_hbm, wkv.at[my_x, my_z, 1]),
+                (win_hbm, win),
+                (wout_hbm, wout),
+                (fgain_hbm, fgain_ref),
+            )
+        )
+    ]
+    for load in loads:
+        load.start()
 
     barrier = pltpu.get_barrier_semaphore()
 
@@ -86,6 +113,12 @@
     lax.fori_loop(1, n_exp, greet, 0)
     for i in range(1, 4):
         pl.semaphore_signal(barrier, inc=1, device_id=((g + i) % 4, d), device_id_type=MESH)
+
+    def arrived(ref, sem):
+        pltpu.make_async_copy(ref, ref, sem).wait()
+
+    loads[0].wait()
+    loads[1].wait()
 
     blk = 16
     qcols = pl.ds(pl.multiple_of(g * quarter, 128), quarter)
@@ -105,34 +138,42 @@
     if prow > rows:
         normed[rows:, :] = jnp.zeros((prow - rows, quarter), BF16)
 
-    pos = lax.broadcasted_iota(jnp.int32, (rows, 1), 0)
-    live = jnp.zeros((rows, 1), jnp.bool_)
-    for s in range(sent):
-        live = live | ((pos >= s * length) & (pos < s * length + lens_ref[s]))
-    lane = lax.broadcasted_iota(jnp.int32, (rows, 128), 1)
+    def along(ref, k):
+        return jnp.concatenate([ref[i, k : k + 1, :] for i in range(sent)], axis=1)
+
+    pos = lax.broadcasted_iota(jnp.int32, (1, rows), 1)
+    live = jnp.zeros((1, rows), jnp.bool_)
+    for i in range(sent):
+        live = live | ((pos >= i * length) & (pos < i * length + lens_ref[i]))
+    expert = lax.broadcasted_iota(jnp.int32, (n_exp, rows), 0)
     earlier = (
         lax.broadcasted_iota(jnp.int32, (rows, rows), 0)
-        > lax.broadcasted_iota(jnp.int32, (rows, rows), 1)
+        < lax.broadcasted_iota(jnp.int32, (rows, rows), 1)
     ).astype(BF16)
     codes = []
-    offset = jnp.zeros((1, 128), F32)
+    offset = jnp.zeros((n_exp, 1), F32)
     for k in range(2):
-        hot = jnp.where((ids_ref[:, k : k + 1] == lane) & live, 1.0, 0.0).astype(F32)
-        rank = jnp.dot(earlier, hot.astype(BF16), preferred_element_type=F32) + offset
-        offset = offset + jnp.sum(hot, axis=0, keepdims=True)
+        hot = jnp.where((along(ids_ref, k) == expert) & live, 1.0, 0.0).astype(F32)
+        rank = jnp.dot(hot.astype(BF16), earlier, preferred_element_type=F32) + offset
+        offset = offset + jnp.sum(hot, axis=1, keepdims=True)
         code = jnp.sum(
-            hot * (rank + (2 * CAPACITY) * lane.astype(F32)), axis=1, keepdims=True
+            hot * (rank + (2 * CAPACITY) * expert.astype(F32)), axis=0, keepdims=True
         )
         codes.append(jnp.where(live, code, -100.0))
-    cols = jnp.where(lane == 0, codes[0], jnp.where(lane == 1, codes[1], -100.0))
+    line = lax.broadcasted_iota(jnp.int32, (128, rows), 0)
+    facts = jnp.zeros((128, rows), F32)
+    for i, fact in enumerate(codes + [along(gates_ref, 0), along(gates_ref, 1)]):
+        facts = jnp.where(line == i, fact, facts)
     if prow > rows:
-        cols = jnp.concatenate([cols, jnp.full((prow - rows, 128), -100.0, F32)], axis=0)
-    trow = cols.T.astype(jnp.int32)
-    row0, row1 = trow[0:1, :], trow[1:2, :]
-    code0, code1 = codes[0].astype(jnp.int32), codes[1].astype(jnp.int32)
-    gate0, gate1 = gates_ref[:, 0:1], gates_ref[:, 1:2]
-
-    pl.semaphore_wait(barrier, n_exp - 1 + 3)
+        facts = jnp.concatenate([facts, jnp.zeros((128, prow - rows), F32)], axis=1)
+        codes = [
+            jnp.concatenate([v, jnp.full((1, prow - rows), -100.0, F32)], axis=1) for v in codes
+        ]
+    row0, row1 = codes[0].astype(jnp.int32), codes[1].astype(jnp.int32)
+    columns = facts.T
+    code0 = columns[:rows, 0:1].astype(jnp.int32)
+    code1 = columns[:rows, 1:2].astype(jnp.int32)
+    gate0, gate1 = columns[:rows, 2:3], columns[:rows, 3:4]
 
     for c in range(n_x):
         base = ((my_x + c) % n_x) * mrow
@@ -146,6 +187,10 @@
             )
         dispatch[c] = acc.astype(BF16).reshape(per, 2 * CAPACITY, half)
 
+    pl.semaphore_wait(barrier, n_exp - 1 + 3)
+
+    for c in range(n_x):
+
         def send(j, carry, c=c):
             z = (my_z + j) % per
             pltpu.make_async_remote_copy(
@@ -166,6 +211,73 @@
         else:
             lax.fori_loop(0, per, send, 0)
 
+    n_z = per // 2
+    my_zz, my_core = my_z // 2, my_z % 2
+    kv_sends = []
+
+    def kv_copy(ref, send_sem, recv_sem, to_x, to_z):
+        cp = pltpu.make_async_remote_copy(
+            src_ref=ref,
+            dst_ref=ref,
+            send_sem=send_sem,
+            recv_sem=recv_sem,
+            device_id=(g, to_x * per + to_z),
+            device_id_type=MESH,
+        )
+        cp.start()
+        kv_sends.append(cp)
+
+    loads[2].wait()
+    loads[3].wait()
+    for i in range(1, n_x):
+        kv_copy(
+            wkv.at[my_x, my_z],
+            kvx_send.at[i],
+            kvx_recv.at[i],
+            (my_x + i) % n_x,
+            my_z,
+        )
+
+    def kv_piece(way, step, core):
+        shift = step if way == 1 else n_z - step
+        z = 2 * ((my_zz + shift) % n_z) + core
+        if step < n_z // 2 or step == 0:
+            return wkv.at[:, z]
+        return wkv.at[:, z, way]
+
+    def kv_event(step):
+        if step > n_z // 2:
+            return
+        other = 2 * my_zz + (1 - my_core)
+        if step == 0:
+            for i in range(1, n_x):
+                arrived(wkv.at[(my_x + n_x - i) % n_x, my_z], kvx_recv.at[i])
+            kv_copy(kv_piece(0, 0, my_core), kvc_send.at[0, 0], kvc_recv.at[0, 0], my_x, other)
+        for way in range(2):
+            if step > 0:
+                arrived(kv_piece(way, step, my_core), kvz_recv.at[way, step])
+            if step < n_z // 2:
+                ref = kv_piece(way, step, my_core)
+                if step + 1 == n_z // 2:
+                    shift = step if way == 1 else n_z - step
+                    ref = wkv.at[:, 2 * ((my_zz + shift) % n_z) + my_core, way]
+                to = 2 * ((my_zz + (1 if way == 0 else n_z - 1)) % n_z) + my_core
+                kv_copy(ref, kvz_send.at[way, step], kvz_recv.at[way, step + 1], my_x, to)
+            if step > 0:
+                kv_copy(
+                    kv_piece(way, step, my_core),
+                    kvc_send.at[way, step],
+                    kvc_recv.at[way, step],
+                    my_x,
+                    other,
+                )
+
+    def kv_finish():
+        arrived(kv_piece(0, 0, 1 - my_core), kvc_recv.at[0, 0])
+        for step in range(1, n_z // 2 + 1):
+            for way in range(2):
+                arrived(kv_piece(way, step, 1 - my_core), kvc_recv.at[way, step])
+
     for c in range(n_x):
         base = ((my_x + c) % n_x) * mrow
         col = lax.broadcasted_iota(jnp.int32, (rows, mrow), 1) + base
@@ -193,9 +305,6 @@
 
     def xs(q, c, start=0, size=per):
         return xbuf.at[q, pl.ds(slab(c) + start, size)]
-
-    def arrived(ref, sem):
-        pltpu.make_async_copy(ref, ref, sem).wait()
 
     hp = per // 2
     sends = []
@@ -235,7 +344,7 @@
                     .astype(BF16)
                 )
         if c == 0:
-            load_in.wait()
+            loads[4].wait()
         tile = min(256, hid.shape[1])
 
         def first(n, carry):
@@ -247,7 +356,7 @@
 
         lax.fori_loop(0, hid.shape[1] // tile, first, 0)
         if c == 0:
-            load_out.wait()
+            loads[5].wait()
 
         def second(q):
             cs = pl.ds(pl.multiple_of(q * quarter, 128), quarter)
@@ -311,6 +420,28 @@
         for k in reversed(range(len(stages))):
             if 0 <= step - k < n_x:
                 stages[k](step - k)
+        kv_event(step)
+
+    kv_finish()
+    columns_kv = wkv.shape[-1]
+    heads = columns_kv // HEAD_DIM
+    pairs = sent * heads
+    row = lax.broadcasted_iota(jnp.int32, (pairs, columns_kv), 0)
+    own_head = row % heads == lax.broadcasted_iota(jnp.int32, (pairs, columns_kv), 1) // HEAD_DIM
+    query = jnp.zeros((pairs, columns_kv), F32)
+    for i in range(sent):
+        query = jnp.where(row // heads == i, query_ref[i : i + 1, :].astype(F32), query)
+    query = jnp.where(own_head, query, 0.0).astype(BF16)
+
+    def projection(kv):
+        return wkv[:, :, kv].reshape(width, columns_kv)
+
+    through = lax.dot_general(
+        query, projection(0), (((1,), (1,)), ((), ())), preferred_element_type=F32
+    )
+    high = through.astype(BF16)
+    qkey[:pairs, :] = high.astype(F32)
+    qkey[pairs:, :] = through - high.astype(F32)
 
     acc = jnp.zeros((4 * rows, half), F32)
     for c in range(n_x):
@@ -347,9 +478,36 @@
         out_ref[r, :] = (cen * lax.rsqrt(var + EPSILON) * fgain_ref[...]).astype(BF16)
         return carry
 
+    loads[6].wait()
     lax.fori_loop(0, rows // blk, final_block, 0)
 
-    for cp in sends:
+    scores = lax.dot_general(
+        qkey[...].astype(BF16), out_ref[...], (((1,), (1,)), ((), ())), preferred_element_type=F32
+    )
+    scores = (scores[:pairs] + scores[pairs:]) * (1.0 / math.sqrt(HEAD_DIM))
+    which = lax.broadcasted_iota(jnp.int32, (pairs, rows), 0) // heads
+    at = lax.broadcasted_iota(jnp.int32, (pairs, rows), 1)
+    inside = jnp.zeros((pairs, rows), jnp.bool_)
+    for i in range(sent):
+        inside = inside | (
+            (which == i) & (at >= i * length) & (at < i * length + lens_ref[i])
+        )
+    weights = jnp.where(inside, jnp.exp(scores), 0.0)
+    probabilities = (weights / jnp.sum(weights, axis=-1, keepdims=True)).astype(BF16)
+    mean_state = jnp.dot(probabilities, out_ref[...], preferred_element_type=F32)
+    high = mean_state.astype(BF16)
+    low = (mean_state - high.astype(F32)).astype(BF16)
+    values = projection(1)
+    context = jnp.dot(high, values, preferred_element_type=F32) + jnp.dot(
+        low, values, preferred_element_type=F32
+    )
+    context = jnp.where(own_head, context, 0.0)
+    for i in range(sent):
+        context_ref[i : i + 1, :] = jnp.sum(
+            jnp.where(row // heads == i, context, 0.0), axis=0, keepdims=True
+        ).astype(BF16)
+
+    for cp in sends + kv_sends:
         cp.wait_send()
     for c in range(n_x):
         count = per - 1 if c == 0 else per
@@ -357,26 +515,52 @@
             arrived(buf.at[c, pl.ds(0, count)], sem.at[c])
 
 
-def experts_layer(n_exp, enc, ngain, fgain, ids, gates, lens, w_in, w_out):
-    rows, width = enc.shape
-    n_x = 4 if n_exp >= 16 else 2
+def on_device(
+    n_exp,
+    enc_states,
+    norm_gain,
+    final_gain,
+    expert_ids,
+    expert_gates,
+    source_lengths,
+    w_in,
+    w_out,
+    w_key,
+    w_value,
+    cross_query,
+):
+    sent, length, width = enc_states.shape
+    rows = sent * length
+    n_x = 4 if n_exp > 16 else 16 // n_exp if n_exp < 16 else 1
+    n_x = min(n_x, n_exp // 2)
     per = n_exp // n_x
+    n_z = per // 2
     quarter, half = width // 4, width // 8
     crow, mrow = per * CAPACITY, per * 2 * CAPACITY
-    ff = w_in.shape[1]
+    ff = w_in.shape[2]
+    kv_rows, kv_columns = w_key.shape
+    pairs = sent * (kv_columns // HEAD_DIM)
     prow = -(-rows // 128) * 128
     vmem = pl.BlockSpec(memory_space=pltpu.VMEM)
-    hbm = pl.BlockSpec(memory_space=pl.ANY)
+    hbm = pl.BlockSpec(memory_space=pltpu.HBM)
     smem = pl.BlockSpec(memory_space=pltpu.SMEM)
     dma = pltpu.SemaphoreType.DMA
-    return pl.pallas_call(
-        functools.partial(moe_kernel, n_exp, n_x),
-        out_shape=jax.ShapeDtypeStruct((rows, width), BF16),
-        in_specs=[vmem, vmem, vmem, vmem, vmem, smem, hbm, hbm],
-        out_specs=vmem,
+    encoded, context = pl.pallas_call(
+        functools.partial(layer_kernel, n_exp, n_x),
+        out_shape=(
+            jax.ShapeDtypeStruct((rows, width), BF16),
+            jax.ShapeDtypeStruct(cross_query.shape, BF16),
+        ),
+        in_specs=[smem, vmem, vmem, vmem] + [hbm] * 7,
+        out_specs=(vmem, vmem),
         scratch_shapes=[
-            pltpu.VMEM(w_in.shape, BF16),
-            pltpu.VMEM(w_out.shape, BF16),
+            pltpu.VMEM((rows, width), BF16),
+            pltpu.VMEM((1, width), F32),
+            pltpu.VMEM((1, width), F32),
+            pltpu.VMEM((n_x, per, 2, kv_rows, kv_columns), BF16),
+            pltpu.VMEM(w_in.shape[1:], BF16),
+            pltpu.VMEM(w_out.shape[1:], BF16),
+            pltpu.VMEM((2 * pairs, width), F32),
             pltpu.VMEM((prow, quarter), BF16),
             pltpu.VMEM((n_x, per, 2 * CAPACITY, half), BF16),
             pltpu.VMEM((4, n_exp, 2 * CAPACITY, half), BF16),
@@ -391,7 +575,7 @@
             pltpu.VMEM((n_x, per, 2 * CAPACITY, half), BF16),
             pltpu.VMEM((n_exp, 2 * CAPACITY, half), BF16),
             pltpu.VMEM((4, rows, quarter), BF16),
-            dma((2,)),
+            dma((7,)),
             dma((n_x,)),
             dma((n_x,)),
             dma((n_x, 4)),
@@ -402,69 +586,35 @@
             dma((n_x,)),
             dma((4,)),
             dma((4,)),
+            dma((n_x,)),
+            dma((n_x,)),
+            dma((2, n_z // 2 + 1)),
+            dma((2, n_z // 2 + 1)),
+            dma((2, n_z // 2 + 1)),
+            dma((2, n_z // 2 + 1)),
         ],
         compiler_params=pltpu.CompilerParams(
-            collective_id=0, has_side_effects=True, vmem_limit_bytes=48 * 1024 * 1024
+            collective_id=0, has_side_effects=True, vmem_limit_bytes=56 * 1024 * 1024
         ),
         cost_estimate=pl.CostEstimate(
             flops=4 * n_exp * CAPACITY * width * ff,
-            bytes_accessed=200_000_000,
+            bytes_accessed=12_000_000,
             transcendentals=0,
         ),
-    )(enc, ngain, fgain, ids, gates, lens, w_in, w_out)
-
-
-def on_device(
-    n_exp,
-    enc_states,
-    norm_gain,
-    final_gain,
-    expert_ids,
-    expert_gates,
-    source_lengths,
-    w_in,
-    w_out,
-    w_key,
-    w_value,
-    cross_query,
-):
-    sentences, length, model_width = enc_states.shape
-    row_count = sentences * length
-    key_rows = lax.all_gather(w_key, "dev", axis=0, tiled=True)
-    value_rows = lax.all_gather(w_value, "dev", axis=0, tiled=True)
-    encoded = experts_layer(
-        n_exp,
-        enc_states.reshape(row_count, model_width),
-        norm_gain.reshape(1, model_width),
-        final_gain.reshape(1, model_width),
-        expert_ids.reshape(row_count, 2),
-        expert_gates.reshape(row_count, 2),
+    )(
         source_lengths,
+        expert_ids.transpose(0, 2, 1),
+        expert_gates.transpose(0, 2, 1),
+        cross_query,
+        enc_states.reshape(rows, width),
+        norm_gain.reshape(1, width),
+        final_gain.reshape(1, width),
+        w_key,
+        w_value,
         w_in[0],
         w_out[0],
     )
-    positions = lax.broadcasted_iota(jnp.int32, (sentences, length), 1)
-    live_mask = positions < source_lengths[:, None]
-    column_count = w_key.shape[1]
-    key_sum = jnp.dot(encoded, key_rows, preferred_element_type=jnp.float32)
-    value_sum = jnp.dot(encoded, value_rows, preferred_element_type=jnp.float32)
-    head_dim = model_width // HEADS
-    local_heads = column_count // head_dim
-    key_cache = key_sum.astype(jnp.bfloat16).reshape(sentences, length, local_heads, head_dim)
-    value_cache = value_sum.astype(jnp.bfloat16).reshape(sentences, length, local_heads, head_dim)
-    queries = cross_query.reshape(sentences, local_heads, head_dim)
-    scores = jnp.einsum("shd,sthd->sht", queries, key_cache, preferred_element_type=jnp.float32) * (
-        1.0 / math.sqrt(head_dim)
-    )
-    weights = jnp.exp(scores) * live_mask[:, None, :].astype(jnp.float32)
-    probabilities = (weights / jnp.sum(weights, axis=-1, keepdims=True)).astype(jnp.bfloat16)
-    context = jnp.einsum(
-        "sht,sthd->shd", probabilities, value_cache, preferred_element_type=jnp.float32
-    )
-    return (
-        encoded.reshape(sentences, length, model_width),
-        context.astype(jnp.bfloat16).reshape(sentences, column_count),
-    )
+    return encoded.reshape(sent, length, width), context
 
 
 def solution(mesh):

time: 183 us -> 92.1 us (0.50)
  waiting for transfers between devices: 70.2 us -> 0 us
  between operations: 14.1 us -> 0.64 us
  local copies, waits for them, and re-layouts: 9.23 us -> 3.34 us
  matrix products: 4.71 us -> 0 us
  Pallas kernels: 83.7 us -> 87.9 us
    all_gather x2 -> x0, waiting for transfers between devices: 68.9 us -> none  [the longest x1 68.9 us: on_device(): value_rows = lax.all_gather(w_value, 'dev', axis=0, tiled=True)]
    unnamed x14 -> x2, local copies, waits for them, and re-layouts: 8.43 us -> 3.34 us
    dot_general x4 -> x0, matrix products: 4.71 us -> none  [the longest x1 2.17 us: on_device(): key_sum = jnp.dot(encoded, key_rows, preferred_element_type=jnp.float32)]
    pallas_call x1, Pallas kernels: 83.7 us -> 87.9 us  [on_device(): pl.pallas_call(functools.partial(layer_kernel, n_exp, n_x), out_shape=(ja...]
  transfers between devices with their start and end apart: 2 -> 0, of which waited for: 1 -> 0; matrix products, arithmetic and copies ran while one was open for 3% -> 0% of each run, Pallas kernels for 46% -> 0%
where the time goes in v2:
time: 92.1 us; the launch traced here: 91.9 us
  Pallas kernels  87.9 us (95%)
  local copies, waits for them, and re-layouts  3.34 us (4%)
    pallas_call x1, Pallas kernels, on_device(): pl.pallas_call(functools.partial(layer_kernel, n_exp, n_x), out_shape=(ja...  87.9 us
    unnamed x2, local copies, waits for them, and re-layouts  3.34 us

profile of v2, /device:TPU:1, one launch (start us, length us, event | category | flops | bytes accessed | tf_op | source)
XLA Modules:
  0.0 91.9 jit_solution(10068876450595407660)
XLA Ops:
  0.6 87.9 %shard_map.122 = (bf16[192,2048]{1,0:T(8,128)(2,1)}, bf16[2,512]{1,0:T(2,128)(2,1)}) custom-call(s32[2]{0:T(128)} %lens_ref.1, s32[2,2,96]{2,1,0:T(2,128)} %bitcast.14, f32[2,2,96]{2,1,0:T(2,128)} %bitcast.15, bf16[2,512]{1,0:T(2,128)(2,1)} %query_ref.1, bf16[192,2048]{1,0:T(8,128)(2,1)} %bitcast.11, f32[1,2048]{1,0:T(1,128)} %bitcast.12, ...), custom_call_target="tpu_custom_call" | custom-call | flops 4294967296 | bytes 12000000 | tf_op jit(solution)/shard_map/pallas_call | solution.py:548
  88.5 2.1 %copy.15 = bf16[2,96,2048]{2,1,0:T(8,128)(2,1)} copy(bf16[2,96,2048]{2,1,0:T(8,128)(2,1)} %bitcast.8) | data formatting | bytes 1572864
  90.6 1.3 %copy.16 = bf16[2,512]{1,0:T(2,128)(2,1)} copy(bf16[2,512]{1,0:T(2,128)(2,1)} %get-tuple-element.9) | data formatting | bytes 4096

commit v3 on v2

--- a/solution.py
+++ b/solution.py
@@ -11,6 +11,14 @@
 HEADS = 16
 HEAD_DIM = 128
 CAPACITY = 8
+AHEAD = 3
+ORDER = (
+    ("a", 0), ("a", 1), ("k", 0), ("b", 0), ("a", 2), ("b", 1),
+    ("a", 3), ("c", 0), ("b", 2), ("c", 1), ("d", 0), ("k", 1),
+    ("b", 3), ("c", 2), ("d", 1), ("k", 2), ("e", 0), ("c", 3),
+    ("d", 2), ("k", 3), ("e", 1), ("d", 3), ("e", 2), ("k", 4),
+    ("e", 3),
+)
 EPSILON = 1e-05
 F32 = jnp.float32
 BF16 = jnp.bfloat16
@@ -189,9 +197,8 @@
 
     pl.semaphore_wait(barrier, n_exp - 1 + 3)
 
-    for c in range(n_x):
-
-        def send(j, carry, c=c):
+    def dispatch_chunk(c):
+        def send(j, carry):
             z = (my_z + j) % per
             pltpu.make_async_remote_copy(
                 src_ref=dispatch.at[c, z],
@@ -210,6 +217,9 @@
             lax.fori_loop(1, per, send, 0)
         else:
             lax.fori_loop(0, per, send, 0)
+
+    for c in range(min(AHEAD, n_x)):
+        dispatch_chunk(c)
 
     n_z = per // 2
     my_zz, my_core = my_z // 2, my_z % 2
@@ -311,6 +321,8 @@
 
     def stage_a(c):
         arrived(xs(g, c), a2a_recv.at[c])
+        if c + AHEAD < n_x:
+            dispatch_chunk(c + AHEAD)
         for i, to in enumerate((right, left)):
             cp = ycopy(xs(g, c), xs(g, c), yag_send.at[c, i], yag_recv.at[c, i], to)
             cp.start()
@@ -415,12 +427,10 @@
         else:
             lax.fori_loop(0, per, send, 0)
 
-    stages = (stage_a, stage_b, stage_c, stage_d, stage_e)
-    for step in range(n_x + len(stages) - 1):
-        for k in reversed(range(len(stages))):
-            if 0 <= step - k < n_x:
-                stages[k](step - k)
-        kv_event(step)
+    stages = dict(a=stage_a, b=stage_b, c=stage_c, d=stage_d, e=stage_e, k=kv_event)
+    for name, index in ORDER:
+        if name == "k" or index < n_x:
+            stages[name](index)
 
     kv_finish()
     columns_kv = wkv.shape[-1]
@@ -455,18 +465,33 @@
     ).astype(BF16)
 
     hm = rows // 2
-    for i, to in enumerate((right, left)):
-        cp = ycopy(mix.at[g], mix.at[g], mix_send.at[i], mix_recv.at[i], to)
+
+    def mix_part(q, i):
+        return mix.at[q, pl.ds(i * hm, hm)]
+
+    for turn in range(2):
+        for way, to in enumerate((right, left)):
+            i = (way + turn) % 2
+            cp = ycopy(
+                mix_part(g, i), mix_part(g, i), mix_send.at[way, i], mix_recv.at[way, i], to
+            )
+            cp.start()
+            sends.append(cp)
+    for way, (origin, to) in enumerate(((left, right), (right, left))):
+        arrived(mix_part(origin, way), mix_recv.at[way, way])
+        cp = ycopy(
+            mix_part(origin, way),
+            mix_part(origin, way),
+            mix_send.at[way, 2],
+            mix_recv.at[way, 2],
+            to,
+        )
         cp.start()
         sends.append(cp)
-    for i, (origin, to) in enumerate(((left, right), (right, left))):
-        arrived(mix.at[origin], mix_recv.at[i])
-        piece = mix.at[origin, pl.ds(i * hm, hm)]
-        cp = ycopy(piece, piece, mix_send.at[2 + i], mix_recv.at[2 + i], to)
-        cp.start()
-        sends.append(cp)
-    for i in range(2):
-        arrived(mix.at[diag, pl.ds(i * hm, hm)], mix_recv.at[2 + i])
+    for way, origin in enumerate((left, right)):
+        arrived(mix_part(origin, 1 - way), mix_recv.at[way, 1 - way])
+    for way in range(2):
+        arrived(mix_part(diag, way), mix_recv.at[way, 2])
 
     def final_block(i, carry):
         r = pl.ds(pl.multiple_of(i * blk, blk), blk)
@@ -479,7 +504,7 @@
         return carry
 
     loads[6].wait()
-    lax.fori_loop(0, rows // blk, final_block, 0)
+    lax.fori_loop(0, rows // blk, final_block, 0, unroll=2)
 
     scores = lax.dot_general(
         qkey[...].astype(BF16), out_ref[...], (((1,), (1,)), ((), ())), preferred_element_type=F32
@@ -513,6 +538,10 @@
         count = per - 1 if c == 0 else per
         for buf, sem in ((dispatch, a2a_send), (back, ret_send)):
             arrived(buf.at[c, pl.ds(0, count)], sem.at[c])
+
+
+def in_hbm(array):
+    return pltpu.with_memory_space_constraint(array, pltpu.HBM)
 
 
 def on_device(
@@ -531,8 +560,7 @@
 ):
     sent, length, width = enc_states.shape
     rows = sent * length
-    n_x = 4 if n_exp > 16 else 16 // n_exp if n_exp < 16 else 1
-    n_x = min(n_x, n_exp // 2)
+    n_x = 1 if n_exp == 16 else min(4, n_exp // 2)
     per = n_exp // n_x
     n_z = per // 2
     quarter, half = width // 4, width // 8
@@ -584,8 +612,8 @@
             dma((n_x, 4)),
             dma((n_x,)),
             dma((n_x,)),
-            dma((4,)),
-            dma((4,)),
+            dma((2, 3)),
+            dma((2, 3)),
             dma((n_x,)),
             dma((n_x,)),
             dma((2, n_z // 2 + 1)),
@@ -594,7 +622,7 @@
             dma((2, n_z // 2 + 1)),
         ],
         compiler_params=pltpu.CompilerParams(
-            collective_id=0, has_side_effects=True, vmem_limit_bytes=56 * 1024 * 1024
+            collective_id=0, has_side_effects=True, vmem_limit_bytes=40 * 1024 * 1024
         ),
         cost_estimate=pl.CostEstimate(
             flops=4 * n_exp * CAPACITY * width * ff,
@@ -602,17 +630,17 @@
             transcendentals=0,
         ),
     )(
-        source_lengths,
-        expert_ids.transpose(0, 2, 1),
-        expert_gates.transpose(0, 2, 1),
-        cross_query,
-        enc_states.reshape(rows, width),
-        norm_gain.reshape(1, width),
-        final_gain.reshape(1, width),
-        w_key,
-        w_value,
-        w_in[0],
-        w_out[0],
+        in_hbm(source_lengths),
+        in_hbm(expert_ids.transpose(0, 2, 1)),
+        in_hbm(expert_gates.transpose(0, 2, 1)),
+        in_hbm(cross_query),
+        in_hbm(enc_states.reshape(rows, width)),
+        in_hbm(norm_gain.reshape(1, width)),
+        in_hbm(final_gain.reshape(1, width)),
+        in_hbm(w_key),
+        in_hbm(w_value),
+        in_hbm(w_in[0]),
+        in_hbm(w_out[0]),
     )
     return encoded.reshape(sent, length, width), context
 

time: 92.1 us -> 83.2 us (0.903)
  Pallas kernels: 87.9 us -> 80.6 us
  local copies, waits for them, and re-layouts: 3.34 us -> 1.46 us
    pallas_call x1, Pallas kernels: 87.9 us -> 80.6 us  [on_device(): pl.pallas_call(functools.partial(layer_kernel, n_exp, n_x), out_shape=(ja...]
    unnamed x2, local copies, waits for them, and re-layouts: 3.34 us -> 1.46 us
where the time goes in v3:
time: 83.2 us; the launch traced here: 82.7 us
  Pallas kernels  80.6 us (97%)
  local copies, waits for them, and re-layouts  1.46 us (2%)
    pallas_call x1, Pallas kernels, on_device(): pl.pallas_call(functools.partial(layer_kernel, n_exp, n_x), out_shape=(ja...  80.6 us

profile of v3, /device:TPU:1, one launch (start us, length us, event | category | flops | bytes accessed | tf_op | source)
XLA Modules:
  0.0 82.7 jit_solution(3015019145032965116)
XLA Ops:
  0.6 80.6 %shard_map.122 = (bf16[192,2048]{1,0:T(8,128)(2,1)S(1)}, bf16[2,512]{1,0:T(2,128)(2,1)S(1)}) custom-call(s32[2]{0:T(128)} %lens_ref.1, s32[2,2,96]{2,1,0:T(2,128)} %bitcast.14, f32[2,2,96]{2,1,0:T(2,128)} %bitcast.15, bf16[2,512]{1,0:T(2,128)(2,1)} %query_ref.1, bf16[192,2048]{1,0:T(8,128)(2,1)} %bitcast.11, f32[1,2048]{1,0:T(1,128)} %bitcast.12, ...), custom_call_target="tpu_custom_call" | custom-call | flops 4294967296 | bytes 12000000 | tf_op jit(solution)/shard_map/pallas_call | solution.py:576
  81.3 0.9 %copy.15 = bf16[2,96,2048]{2,1,0:T(8,128)(2,1)} copy(bf16[2,96,2048]{2,1,0:T(8,128)(2,1)S(1)} %bitcast.8) | data formatting | bytes 1572864
  82.2 0.6 copy.16

commit v4 on v3

--- a/solution.py
+++ b/solution.py
@@ -12,12 +12,13 @@
 HEAD_DIM = 128
 CAPACITY = 8
 AHEAD = 3
+UNROLL = 6
 ORDER = (
-    ("a", 0), ("a", 1), ("k", 0), ("b", 0), ("a", 2), ("b", 1),
-    ("a", 3), ("c", 0), ("b", 2), ("c", 1), ("d", 0), ("k", 1),
-    ("b", 3), ("c", 2), ("d", 1), ("k", 2), ("e", 0), ("c", 3),
-    ("d", 2), ("k", 3), ("e", 1), ("d", 3), ("e", 2), ("k", 4),
-    ("e", 3),
+    ("a", 0), ("a", 1), ("k", 0), ("b", 0), ("a", 2), ("p", 0),
+    ("b", 1), ("a", 3), ("c", 0), ("p", 1), ("b", 2), ("c", 1),
+    ("p", 2), ("d", 0), ("k", 1), ("b", 3), ("c", 2), ("p", 3),
+    ("d", 1), ("k", 2), ("e", 0), ("c", 3), ("d", 2), ("k", 3),
+    ("e", 1), ("d", 3), ("e", 2), ("k", 4), ("e", 3),
 )
 EPSILON = 1e-05
 F32 = jnp.float32
@@ -54,6 +55,7 @@
     combine,
     xrow,
     hid,
+    hidden_sum,
     part,
     st1,
     rv1,
@@ -344,29 +346,49 @@
 
     hrow = crow // 2
 
+    tile = min(256, hid.shape[1])
+
+    def place(k, q, c):
+        block = xbuf[q, pl.ds(slab(c), per)].astype(F32)
+        for h in range(2):
+            xrow[:, k * quarter + h * half : k * quarter + (h + 1) * half] = (
+                block[:, h * CAPACITY : (h + 1) * CAPACITY, :].reshape(crow, half).astype(BF16)
+            )
+
+    def term(k, q, cs):
+        features = pl.ds(pl.multiple_of(q * quarter, 128), quarter)
+        return jnp.dot(
+            xrow[:, k * quarter : (k + 1) * quarter],
+            win[features, cs],
+            preferred_element_type=F32,
+        )
+
+    def stage_p(c):
+        if c == 0:
+            loads[4].wait()
+        early = (g, left, right)
+        for k, q in enumerate(early):
+            place(k, q, c)
+
+        def add_early(n, carry):
+            cs = pl.ds(pl.multiple_of(n * tile, tile), tile)
+            hidden_sum[c, :, cs] = term(0, g, cs) + term(1, left, cs) + term(2, right, cs)
+            return carry
+
+        lax.fori_loop(0, hid.shape[1] // tile, add_early, 0)
+
     def stage_c(c):
         arrived(xs(diag, c, 0, hp), yag_recv.at[c, 2])
         arrived(xs(diag, c, hp, hp), yag_recv.at[c, 3])
-        for q in range(4):
-            block = xbuf[q, pl.ds(slab(c), per)].astype(F32)
-            for h in range(2):
-                xrow[:, q * quarter + h * half : q * quarter + (h + 1) * half] = (
-                    block[:, h * CAPACITY : (h + 1) * CAPACITY, :]
-                    .reshape(crow, half)
-                    .astype(BF16)
-                )
-        if c == 0:
-            loads[4].wait()
-        tile = min(256, hid.shape[1])
-
-        def first(n, carry):
+        place(3, diag, c)
+
+        def add_last(n, carry):
             cs = pl.ds(pl.multiple_of(n * tile, tile), tile)
-            hid[:, cs] = jnp.maximum(
-                jnp.dot(xrow[...], win[:, cs], preferred_element_type=F32), 0.0
-            ).astype(BF16)
+            total = hidden_sum[c, :, cs] + term(3, diag, cs)
+            hid[:, cs] = jnp.maximum(total, 0.0).astype(BF16)
             return carry
 
-        lax.fori_loop(0, hid.shape[1] // tile, first, 0)
+        lax.fori_loop(0, hid.shape[1] // tile, add_last, 0)
         if c == 0:
             loads[5].wait()
 
@@ -427,7 +449,7 @@
         else:
             lax.fori_loop(0, per, send, 0)
 
-    stages = dict(a=stage_a, b=stage_b, c=stage_c, d=stage_d, e=stage_e, k=kv_event)
+    stages = dict(p=stage_p, a=stage_a, b=stage_b, c=stage_c, d=stage_d, e=stage_e, k=kv_event)
     for name, index in ORDER:
         if name == "k" or index < n_x:
             stages[name](index)
@@ -504,7 +526,7 @@
         return carry
 
     loads[6].wait()
-    lax.fori_loop(0, rows // blk, final_block, 0, unroll=2)
+    lax.fori_loop(0, rows // blk, final_block, 0, unroll=UNROLL)
 
     scores = lax.dot_general(
         qkey[...].astype(BF16), out_ref[...], (((1,), (1,)), ((), ())), preferred_element_type=F32
@@ -522,11 +544,10 @@
     mean_state = jnp.dot(probabilities, out_ref[...], preferred_element_type=F32)
     high = mean_state.astype(BF16)
     low = (mean_state - high.astype(F32)).astype(BF16)
-    values = projection(1)
-    context = jnp.dot(high, values, preferred_element_type=F32) + jnp.dot(
-        low, values, preferred_element_type=F32
+    terms = jnp.dot(
+        jnp.concatenate([high, low], axis=0), projection(1), preferred_element_type=F32
     )
-    context = jnp.where(own_head, context, 0.0)
+    context = jnp.where(own_head, terms[:pairs] + terms[pairs:], 0.0)
     for i in range(sent):
         context_ref[i : i + 1, :] = jnp.sum(
             jnp.where(row // heads == i, context, 0.0), axis=0, keepdims=True
@@ -595,6 +616,7 @@
             pltpu.VMEM((n_x, 4 * rows, mrow), BF16),
             pltpu.VMEM((crow, width), BF16),
             pltpu.VMEM((crow, ff), BF16),
+            pltpu.VMEM((n_x, crow, ff), F32),
             pltpu.VMEM((n_x, 3, crow, quarter), F32),
             pltpu.VMEM((n_x, crow, quarter), BF16),
             pltpu.VMEM((n_x, crow, quarter), BF16),

time: 83.2 us -> 81.9 us (0.984)
  Pallas kernels: 80.6 us -> 79.4 us
    pallas_call x1, Pallas kernels: 80.6 us -> 79.4 us  [on_device(): pl.pallas_call(functools.partial(layer_kernel, n_exp, n_x), out_shape=(ja...]
where the time goes in v4:
time: 81.9 us; the launch traced here: 81.5 us
  Pallas kernels  79.4 us (97%)
  local copies, waits for them, and re-layouts  1.46 us (2%)
    pallas_call x1, Pallas kernels, on_device(): pl.pallas_call(functools.partial(layer_kernel, n_exp, n_x), out_shape=(ja...  79.4 us

profile of v4, /device:TPU:1, one launch (start us, length us, event | category | flops | bytes accessed | tf_op | source)
XLA Modules:
  0.0 81.5 jit_solution(2674704936343213685)
XLA Ops:
  0.6 79.4 %shard_map.122 = (bf16[192,2048]{1,0:T(8,128)(2,1)S(1)}, bf16[2,512]{1,0:T(2,128)(2,1)S(1)}) custom-call(s32[2]{0:T(128)} %lens_ref.1, s32[2,2,96]{2,1,0:T(2,128)} %bitcast.14, f32[2,2,96]{2,1,0:T(2,128)} %bitcast.15, bf16[2,512]{1,0:T(2,128)(2,1)} %query_ref.1, bf16[192,2048]{1,0:T(8,128)(2,1)} %bitcast.11, f32[1,2048]{1,0:T(1,128)} %bitcast.12, ...), custom_call_target="tpu_custom_call" | custom-call | flops 4294967296 | bytes 12000000 | tf_op jit(solution)/shard_map/pallas_call | solution.py:597
  80.1 0.9 %copy.15 = bf16[2,96,2048]{2,1,0:T(8,128)(2,1)} copy(bf16[2,96,2048]{2,1,0:T(8,128)(2,1)S(1)} %bitcast.8) | data formatting | bytes 1572864
  80.9 0.6 copy.16

commit v5 on v4

--- a/solution.py
+++ b/solution.py
@@ -432,7 +432,7 @@
         back[c] = jnp.concatenate([total[:, :, :half], total[:, :, half:]], axis=1).astype(BF16)
 
         def send(j, carry):
-            z = (my_z + j) % per
+            z = (my_z + j + (0 if c == 0 else per // 2)) % per
             pltpu.make_async_remote_copy(
                 src_ref=back.at[c, z],
                 dst_ref=ybuf.at[d],

time: 81.9 us -> 81.8 us (level)
  no operation moved by 1% of the time
where the time goes in v5:
time: 81.8 us; the launch traced here: 81.2 us
  Pallas kernels  79.1 us (97%)
  local copies, waits for them, and re-layouts  1.46 us (2%)
    pallas_call x1, Pallas kernels, on_device(): pl.pallas_call(functools.partial(layer_kernel, n_exp, n_x), out_shape=(ja...  79.1 us

profile of v5, /device:TPU:1, one launch (start us, length us, event | category | flops | bytes accessed | tf_op | source)
XLA Modules:
  0.0 81.2 jit_solution(17037852149504952790)
XLA Ops:
  0.6 79.1 %shard_map.122 = (bf16[192,2048]{1,0:T(8,128)(2,1)S(1)}, bf16[2,512]{1,0:T(2,128)(2,1)S(1)}) custom-call(s32[2]{0:T(128)} %lens_ref.1, s32[2,2,96]{2,1,0:T(2,128)} %bitcast.14, f32[2,2,96]{2,1,0:T(2,128)} %bitcast.15, bf16[2,512]{1,0:T(2,128)(2,1)} %query_ref.1, bf16[192,2048]{1,0:T(8,128)(2,1)} %bitcast.11, f32[1,2048]{1,0:T(1,128)} %bitcast.12, ...), custom_call_target="tpu_custom_call" | custom-call | flops 4294967296 | bytes 12000000 | tf_op jit(solution)/shard_map/pallas_call | solution.py:597
  79.7 0.9 %copy.15 = bf16[2,96,2048]{2,1,0:T(8,128)(2,1)} copy(bf16[2,96,2048]{2,1,0:T(8,128)(2,1)S(1)} %bitcast.8) | data formatting | bytes 1572864
  80.6 0.6 copy.16
